TPU v7x, 512 devices: a whole 4x8x8 slice. The times are simulated.
512 devices in a mesh: dp: 64 (over x, z, y_hi), layer: 8 (over y_lo, core).
Axes of the slice: x: 4, y: 8 (y_hi: 2, y_lo: 4; y = y_hi * 4 + y_lo), z: 8, core: 2. Of those that a mesh axis runs over, the one named last changes fastest.
Arguments:
- grad: bfloat16 [16384, 2048], P(('layer', 'dp')), parts along dimension 0, may hold values from -0.59765625 to 0.59765625
- left_gram: float32 [16384, 2048], P(('layer', 'dp')), parts along dimension 0, may hold values from -0.2 to 17
- basis: float32 [16384, 512], P(('layer', 'dp')), parts along dimension 0, may hold values from -6 to 6
- exp_avg: float32 [16384, 512], P(('layer', 'dp')), parts along dimension 0, may hold values from -6 to 6
- exp_avg_sq: float32 [16384, 512], P(('layer', 'dp')), parts along dimension 0, may hold values from 0.01 to 1
Outputs:
- left_gram_new: float32 [16384, 2048], P(('layer', 'dp')), parts along dimension 0
- basis_new: float32 [16384, 512], P(('layer', 'dp')), parts along dimension 0
- exp_avg_new: float32 [16384, 512], P(('layer', 'dp')), parts along dimension 0
- exp_avg_sq_new: float32 [16384, 512], P(('layer', 'dp')), parts along dimension 0
There are 8 independent parts, one for each index of `layer`. A program takes and returns all parts, laid end to end along the dimension named above; each array names one. Nothing has to cross between parts.
All inputs are finite; a program needn't handle non-finite values.
Results may differ from a plain program's by a relative error of at most 0.003.
The roundings to bfloat16 on the way count: a program that leaves them out, or rounds other values in their place, can miss the bound.
Values may be sent and summed in bfloat16 or wider, within the bound.
A program may use at most 64 MiB of HBM per device.

v0:
```python
import functools
import math

import jax
import jax.numpy as jnp
from jax import lax
from jax.experimental import pallas as pl
from jax.experimental.pallas import tpu as pltpu
from jax.sharding import PartitionSpec as P

D = 2048
K = 512
R = 32
HIGHEST = lax.Precision.HIGHEST
F32 = jnp.float32
BF16 = jnp.bfloat16
GA, GB, WA, WB, LG, GN, PP, PG, FR, CR, FA, CA, FB, CB = range(14)


def dot(a, b, dims, precision=None):
    return lax.dot_general(a, b, (dims, ((), ())), precision=precision, preferred_element_type=F32)


def dot3(a, b, dims):
    ah, bh = a.astype(BF16), b.astype(BF16)
    al, bl = (a - ah.astype(F32)).astype(BF16), (b - bh.astype(F32)).astype(BF16)
    return dot(ah, bh, dims) + (dot(ah, bl, dims) + dot(al, bh, dims))


def lane(v, k):
    return jnp.broadcast_to(v[:, k : k + 1], (8, 128))


def sub(v, t):
    return jnp.broadcast_to(v[t : t + 1, :], (8, 128))


def inverse_factor(a_rows):
    row = lax.broadcasted_iota(jnp.int32, (8, 128), 0)
    col = lax.broadcasted_iota(jnp.int32, (8, 128), 1)
    n = len(a_rows)
    a_rows = list(a_rows)
    e_rows = [jnp.where(col == row + 8 * i, 1.0, 0.0).astype(F32) for i in range(n)]
    out = []
    for m in range(n):
        r_m, s_m = a_rows[m], e_rows[m]
        c = [lane(r_m, 8 * m + t) for t in range(8)]
        v = jnp.zeros((8, 128), F32)
        for t in range(8):
            here = row == t
            pivot = sub(c[t], t)
            inv = 1.0 / pivot
            s_t = sub(s_m, t)
            v = jnp.where(here, s_t * lax.rsqrt(pivot), v)
            mult = jnp.where(here, -1.0, c[t])
            for u in range(t + 1, 8):
                c[u] = jnp.where(here, 0.0, c[u]) - mult * (sub(c[u], t) * inv)
            if m < n - 1:
                r_m = jnp.where(here, 0.0, r_m) - mult * (sub(r_m, t) * inv)
                s_m = jnp.where(here, 0.0, s_m) - mult * (s_t * inv)
            elif t < 7:
                s_m = jnp.where(here, 0.0, s_m) - mult * (s_t * inv)
        out.append(v)
        if m < n - 1:
            w = [sub(r_m, t) for t in range(8)]
            s = [sub(s_m, t) for t in range(8)]
            for i in range(m + 1, n):
                l = [lane(a_rows[i], 8 * m + t) for t in range(8)]
                for t in range(8):
                    a_rows[i] = a_rows[i] - l[t] * w[t]
                    e_rows[i] = e_rows[i] - l[t] * s[t]
    return out


def split_columns(lg_ref, out_ref):
    low = lax.broadcasted_iota(jnp.int32, (R, 128), 1) < 64
    for x in range(4):
        t = [lg_ref[:, x * 512 + k * 128 : x * 512 + (k + 1) * 128] for k in range(4)]
        for h in range(2):
            a, b = t[2 * h], t[2 * h + 1]
            out_ref[2 * x, :, h * 128 : (h + 1) * 128] = jnp.where(low, a, pltpu.roll(b, 64, 1))
            out_ref[2 * x + 1, :, h * 128 : (h + 1) * 128] = jnp.where(low, pltpu.roll(a, 64, 1), b)


def join_columns(in_ref, out_ref):
    low = lax.broadcasted_iota(jnp.int32, (R, 128), 1) < 64
    for x in range(4):
        for h in range(2):
            a = in_ref[2 * x, :, h * 128 : (h + 1) * 128]
            b = in_ref[2 * x + 1, :, h * 128 : (h + 1) * 128]
            at = x * 512 + h * 256
            out_ref[:, at : at + 128] = jnp.where(low, a, pltpu.roll(b, 64, 1))
            out_ref[:, at + 128 : at + 256] = jnp.where(low, pltpu.roll(a, 64, 1), b)


def kernel(
    grad_ref, lg_ref, basis_ref, avg_ref, sq_ref,
    lgn_ref, basis_out, avg_out, sq_out,
    ga, gb, wa, wb, lgs, lgr, gn, gback, pp, pr, pb, pt, fp, fr, cp, cr, fall, call, yf, yc, diag, inverse,
    send_sem, recv_sem,
):
    me = lax.axis_index("dp")
    x, z21, z0, yh = me // 16, (me // 4) % 4, (me // 2) % 2, me % 2
    p = x * 2 + z0
    q = z21 * 2 + yh

    def device(pp_, qq_):
        return {"dp": (pp_ // 2) * 16 + (qq_ // 2) * 4 + (pp_ % 2) * 2 + qq_ % 2}

    def p_peers():
        return [(p + d) % 8 for d in range(1, 8)]

    def q_peers():
        return [(q + d) % 8 for d in range(1, 8)]

    barrier = pltpu.get_barrier_semaphore()
    for o in p_peers():
        pl.semaphore_signal(barrier, inc=1, device_id=device(o, q), device_id_type=pl.DeviceIdType.MESH)
    for o in q_peers():
        pl.semaphore_signal(barrier, inc=1, device_id=device(p, o), device_id_type=pl.DeviceIdType.MESH)

    def rows(ref, i, n=R):
        return ref.at[pl.ds(pl.multiple_of(i * n, n), n)]

    def copy(phase, src, dst, to, slot_from, dev):
        return pltpu.make_async_remote_copy(
            src_ref=src, dst_ref=dst,
            send_sem=send_sem.at[phase, to], recv_sem=recv_sem.at[phase, slot_from],
            device_id=dev, device_id_type=pl.DeviceIdType.MESH,
        )

    started = []

    def send_p(phase, src, dst):
        for o in p_peers():
            c = copy(phase, src(o), dst(p), o, p, device(o, q))
            c.start()
            started.append(c)

    def send_q(phase, src, dst):
        for o in q_peers():
            c = copy(phase, src(o), dst(q), o, q, device(p, o))
            c.start()
            started.append(c)

    def wait_p(phase, dst):
        for o in p_peers():
            copy(phase, dst(o), dst(o), o, o, device(o, q)).wait_recv()

    def wait_q(phase, dst):
        for o in q_peers():
            copy(phase, dst(o), dst(o), o, o, device(p, o)).wait_recv()

    rows(wa, q)[...] = basis_ref[...].astype(BF16)
    rows(wb, p)[...] = basis_ref[...].astype(BF16)
    pl.semaphore_wait(barrier, 14)
    send_p(GB, lambda o: grad_ref, lambda i: rows(gb, i))
    send_q(GA, lambda o: grad_ref, lambda i: rows(ga, i))
    split_columns(lg_ref, lgs)
    send_p(LG, lambda o: lgs.at[o], lambda i: lgr.at[i])
    send_q(WA, lambda o: rows(wa, q), lambda i: rows(wa, i))
    send_p(WB, lambda o: rows(wb, p), lambda i: rows(wb, i))
    rows(ga, q)[...] = grad_ref[...]
    rows(gb, p)[...] = grad_ref[...]
    lgr[p] = lgs[p]
    wait_p(GB, lambda i: rows(gb, i))
    wait_q(GA, lambda i: rows(ga, i))
    wait_p(LG, lambda i: lgr.at[i])
    gram = dot(gb[...], ga[...], ((1,), (1,)))
    new = 0.95 * lgr[...].reshape(256, 256) + 0.05 * gram
    gn[...] = new.reshape(8, R, 256)
    gback[p] = gn[p]
    wait_q(WA, lambda i: rows(wa, i))
    high = new.astype(BF16)
    rest = new - high.astype(F32)
    mid = rest.astype(BF16)
    low = (rest - mid.astype(F32)).astype(BF16)
    w = wa[...]
    part = dot(high, w, ((1,), (0,))) + (dot(mid, w, ((1,), (0,))) + dot(low, w, ((1,), (0,))))
    pp[...] = part.reshape(8, R, K)
    send_p(PP, lambda o: pp.at[o], lambda i: pr.at[i])
    pr[p] = pp[p]
    wait_p(PP, lambda i: pr.at[i])
    own = pr[0]
    for i in range(1, 8):
        own = own + pr[i]
    rows(pb, p)[...] = own
    send_p(PG, lambda o: rows(pb, p), lambda i: rows(pb, i))
    send_p(GN, lambda o: gn.at[o], lambda i: gback.at[i])
    yf[...] = jnp.zeros_like(yf)
    yc[...] = jnp.zeros_like(yc)
    call[:, K:] = jnp.zeros((K, 128), F32)
    call[:, K : K + R] = own.T
    wait_p(WB, lambda i: rows(wb, i))
    wait_p(PG, lambda i: rows(pb, i))
    pt[...] = pb[...].T
    left = rows(pt, p, 64)[...]
    fp[...] = dot(left, pb[...], ((1,), (0,)), HIGHEST).reshape(8, 8, K)
    send_q(FR, lambda o: fp.at[o], lambda i: fr.at[i])
    cp[...] = dot(left, wb[...].astype(F32), ((1,), (0,)), HIGHEST).reshape(8, 8, K)
    send_q(CR, lambda o: cp.at[o], lambda i: cr.at[i])
    fr[q] = fp[q]
    cr[q] = cp[q]

    def total(ref):
        s = ref[0]
        for i in range(1, 8):
            s = s + ref[i]
        return s

    def crow(i, n=8):
        return call.at[pl.ds(pl.multiple_of(i * n, n), n), pl.ds(0, K)]

    wait_q(FR, lambda i: fr.at[i])
    rows(fall, p * 8 + q, 8)[...] = total(fr)
    send_q(FA, lambda o: rows(fall, p * 8 + q, 8), lambda i: rows(fall, p * 8 + i, 8))
    wait_q(CR, lambda i: cr.at[i])
    crow(p * 8 + q)[...] = total(cr)
    send_q(CA, lambda o: crow(p * 8 + q), lambda i: crow(p * 8 + i))
    wait_q(FA, lambda i: rows(fall, p * 8 + i, 8))
    send_p(FB, lambda o: rows(fall, p, 64), lambda i: rows(fall, i, 64))
    wait_p(GN, lambda i: gback.at[i])
    join_columns(gback, lgn_ref)
    wait_q(CA, lambda i: crow(p * 8 + i))

    def wait_row(phase, ref, i):
        @pl.when(i != p)
        def _():
            copy(phase, ref(i), ref(i), i, i, device(i, q)).wait_recv()

    scale = math.sqrt(D)

    def block(k):
        return pl.ds(pl.multiple_of(k * 128, 128), 128)

    def main_rows(k):
        here = block(k)
        u = yf[:, here]
        a = fall[here, :] - dot(u, yf[...], ((0,), (0,)), HIGHEST)
        diag[...] = fall[here, here] - dot(u, u, ((0,), (0,)), HIGHEST)
        out = inverse_factor([diag[8 * i : 8 * i + 8, :] for i in range(16)])
        for i in range(16):
            inverse[k, 8 * i : 8 * i + 8, :] = out[i]
        yf[here, :] = dot(inverse[k], a, ((1,), (0,)), HIGHEST)

    def side_rows(k):
        here = block(k)
        a = call[here, :] - dot3(yf[:, here], yc[...], ((0,), (0,)))
        y = dot3(inverse[k], a, ((1,), (0,)))
        yc[here, :] = y
        basis_out[:, here] = (scale * y[:, K:]).T[:R, :]
        rotation = y[:, :K] / scale
        avg_out[:, here] = dot3(avg_ref[...], rotation, ((1,), (1,)))
        sq_out[:, here] = dot3(sq_ref[...], rotation * rotation, ((1,), (1,)))

    @pl.loop(0, 2)
    def _(k):
        wait_row(FB, lambda i: rows(fall, i, 64), 2 * k)
        wait_row(FB, lambda i: rows(fall, i, 64), 2 * k + 1)

        @pl.when(k == 0)
        def _():
            for o in p_peers():
                copy(CB, crow(p, 64), crow(p, 64), o, p, device(o, q)).start()

        main_rows(k)

    @pl.loop(2, 4)
    def _(k):
        for h in range(2):
            wait_row(FB, lambda i: rows(fall, i, 64), 2 * k + h)
            wait_row(CB, lambda i: crow(i, 64), 2 * (k - 2) + h)
        side_rows(k - 2)
        main_rows(k)

    for h in range(4, 8):
        wait_row(CB, lambda i: crow(i, 64), h)
    side_rows(2)
    side_rows(3)
    for o in p_peers():
        copy(CB, crow(p, 64), crow(p, 64), o, p, device(o, q)).wait_send()
    for c in started:
        c.wait_send()


def body(grad, left_gram, basis, exp_avg, exp_avg_sq):
    vm = pl.BlockSpec(memory_space=pltpu.VMEM)
    sds = jax.ShapeDtypeStruct
    return pl.pallas_call(
        kernel,
        out_shape=(sds((R, D), F32), sds((R, K), F32), sds((R, K), F32), sds((R, K), F32)),
        in_specs=[vm] * 5,
        out_specs=(vm,) * 4,
        scratch_shapes=[
            pltpu.VMEM((256, D), BF16), pltpu.VMEM((256, D), BF16),
            pltpu.VMEM((256, K), BF16), pltpu.VMEM((256, K), BF16),
            pltpu.VMEM((8, R, 256), F32), pltpu.VMEM((8, R, 256), F32),
            pltpu.VMEM((8, R, 256), F32), pltpu.VMEM((8, R, 256), F32),
            pltpu.VMEM((8, R, K), F32), pltpu.VMEM((8, R, K), F32),
            pltpu.VMEM((256, K), F32), pltpu.VMEM((K, 256), F32),
            pltpu.VMEM((8, 8, K), F32), pltpu.VMEM((8, 8, K), F32),
            pltpu.VMEM((8, 8, K), F32), pltpu.VMEM((8, 8, K), F32),
            pltpu.VMEM((K, K), F32), pltpu.VMEM((K, K + 128), F32),
            pltpu.VMEM((K, K), F32), pltpu.VMEM((K, K + 128), F32),
            pltpu.VMEM((128, 128), F32), pltpu.VMEM((4, 128, 128), F32),
            pltpu.SemaphoreType.DMA((14, 8)), pltpu.SemaphoreType.DMA((14, 8)),
        ],
        compiler_params=pltpu.CompilerParams(
            collective_id=0, has_side_effects=True, vmem_limit_bytes=48 * 1024 * 1024
        ),
        cost_estimate=pl.CostEstimate(flops=1_000_000_000, bytes_accessed=2_000_000, transcendentals=0),
        name="soap_refresh",
    )(grad, left_gram, basis, exp_avg, exp_avg_sq)


def solution(mesh):
    placed = P(("layer", "dp"), None)
    return jax.shard_map(
        body, mesh=mesh, in_specs=(placed,) * 5, out_specs=(placed,) * 4, check_vma=False
    )
```

profile of v0, /device:TPU:84, one launch (start us, length us, event | category | flops | bytes accessed | tf_op | source)
XLA Modules:
  0.0 150.2 jit_solution(5730689953898090723)
XLA Ops:
  0.6 0.0 copy-start
  0.6 0.9 copy-done
  1.6 0.0 copy-start.1
  1.6 0.9 copy-done.1
  2.5 0.0 copy-start.2
  2.5 0.8 copy-done.2
  3.3 0.0 copy-start.3
  3.3 0.8 copy-done.3
  4.2 0.0 copy-start.4
  4.2 0.8 copy-done.4
  5.0 142.6 %soap_refresh.1 = (f32[32,2048]{1,0:T(8,128)S(1)}, f32[32,512]{1,0:T(8,128)S(1)}, f32[32,512]{1,0:T(8,128)S(1)}, f32[32,512]{1,0:T(8,128)S(1)}) custom-call(bf16[32,2048]{1,0:T(8,128)(2,1)S(1)} %copy-done.1, f32[32,2048]{1,0:T(8,128)S(1)} %copy-done, f32[32,512]{1,0:T(8,128)S(1)} %copy-done.2, f32[32,512]{1,0:T(8,128)S(1)} %copy-done.3, f32[32,512]{1,0:T(8,128)S(1)} %copy-done.4), custom_call_target="tpu_custom_call" | custom-call | flops 1000000000 | bytes 2000000 | tf_op jit(solution)/shard_map/soap_refresh/pallas_call | solution.py:289
  147.6 0.7 copy.13
  148.3 0.6 copy.14
  148.9 0.6 copy.15
  149.6 0.6 copy.16
Async XLA Ops:
  0.6 1.0 copy-start
  1.6 0.9 copy-start.1
  2.5 0.8 copy-start.2
  3.3 0.8 copy-start.3
  4.2 0.8 copy-start.4
where the time goes:
time: 151 us; the launch traced here: 150 us
  Pallas kernels  143 us (95%)
  local copies, waits for them, and re-layouts  6.96 us (5%)
    pallas_call x1, Pallas kernels, body(): pl.pallas_call(kernel, out_shape=(sds((R, D), F32), sds((R, K), F32), sds...  143 us
    unnamed x14, local copies, waits for them, and re-layouts  6.96 us

commit v1 on v0

--- a/solution.py
+++ b/solution.py
@@ -14,7 +14,8 @@
 HIGHEST = lax.Precision.HIGHEST
 F32 = jnp.float32
 BF16 = jnp.bfloat16
-GA, GB, WA, WB, LG, GN, PP, PG, FR, CR, FA, CA, FB, CB = range(14)
+LG, GN, PP, PG, FR, CR, FA, CA, FB, CB = range(10)
+WIDE = D + K
 
 
 def dot(a, b, dims, precision=None):
@@ -35,7 +36,7 @@
     return jnp.broadcast_to(v[t : t + 1, :], (8, 128))
 
 
-def inverse_factor(a_rows):
+def inverse_factor(a_rows, hooks={}):
     row = lax.broadcasted_iota(jnp.int32, (8, 128), 0)
     col = lax.broadcasted_iota(jnp.int32, (8, 128), 1)
     n = len(a_rows)
@@ -43,6 +44,7 @@
     e_rows = [jnp.where(col == row + 8 * i, 1.0, 0.0).astype(F32) for i in range(n)]
     out = []
     for m in range(n):
+        hooks.get(m, lambda: None)()
         r_m, s_m = a_rows[m], e_rows[m]
         c = [lane(r_m, 8 * m + t) for t in range(8)]
         v = jnp.zeros((8, 128), F32)
@@ -54,12 +56,12 @@
             v = jnp.where(here, s_t * lax.rsqrt(pivot), v)
             mult = jnp.where(here, -1.0, c[t])
             for u in range(t + 1, 8):
-                c[u] = jnp.where(here, 0.0, c[u]) - mult * (sub(c[u], t) * inv)
+                c[u] = jnp.where(here, 0.0, c[u]) - (mult * sub(c[u], t)) * inv
             if m < n - 1:
-                r_m = jnp.where(here, 0.0, r_m) - mult * (sub(r_m, t) * inv)
-                s_m = jnp.where(here, 0.0, s_m) - mult * (s_t * inv)
+                r_m = jnp.where(here, 0.0, r_m) - (mult * sub(r_m, t)) * inv
+                s_m = jnp.where(here, 0.0, s_m) - (mult * s_t) * inv
             elif t < 7:
-                s_m = jnp.where(here, 0.0, s_m) - mult * (s_t * inv)
+                s_m = jnp.where(here, 0.0, s_m) - (mult * s_t) * inv
         out.append(v)
         if m < n - 1:
             w = [sub(r_m, t) for t in range(8)]
@@ -94,10 +96,11 @@
 
 
 def kernel(
-    grad_ref, lg_ref, basis_ref, avg_ref, sq_ref,
+    grad_hbm, lg_hbm, basis_hbm, avg_hbm, sq_hbm,
     lgn_ref, basis_out, avg_out, sq_out,
-    ga, gb, wa, wb, lgs, lgr, gn, gback, pp, pr, pb, pt, fp, fr, cp, cr, fall, call, yf, yc, diag, inverse,
-    send_sem, recv_sem,
+    lg_ref, basis_ref, avg_ref, sq_ref,
+    ga, gb, lgs, lgr, gn, gback, pp, pr, pb, pt, fp, fr, cp, cr, fall, call, yf, yc, diag, inverse,
+    send_sem, recv_sem, gather_send, gather_recv, in_sem,
 ):
     me = lax.axis_index("dp")
     x, z21, z0, yh = me // 16, (me // 4) % 4, (me // 2) % 2, me % 2
@@ -121,6 +124,23 @@
 
     def rows(ref, i, n=R):
         return ref.at[pl.ds(pl.multiple_of(i * n, n), n)]
+
+    def grad_rows(ref, i):
+        return ref.at[pl.ds(pl.multiple_of(i * R, R), R), pl.ds(0, D)]
+
+    def basis_rows(ref, i):
+        return ref.at[pl.ds(pl.multiple_of(i * R, R), R), pl.ds(D, K)]
+
+    loads = [
+        pltpu.make_async_copy(basis_hbm, basis_ref, in_sem.at[0]),
+        pltpu.make_async_copy(grad_hbm, grad_rows(ga, q), in_sem.at[1]),
+        pltpu.make_async_copy(grad_hbm, grad_rows(gb, p), in_sem.at[2]),
+        pltpu.make_async_copy(lg_hbm, lg_ref, in_sem.at[3]),
+        pltpu.make_async_copy(avg_hbm, avg_ref, in_sem.at[4]),
+        pltpu.make_async_copy(sq_hbm, sq_ref, in_sem.at[5]),
+    ]
+    for c in loads:
+        c.start()
 
     def copy(phase, src, dst, to, slot_from, dev):
         return pltpu.make_async_remote_copy(
@@ -151,62 +171,129 @@
         for o in q_peers():
             copy(phase, dst(o), dst(o), o, o, device(p, o)).wait_recv()
 
-    rows(wa, q)[...] = basis_ref[...].astype(BF16)
-    rows(wb, p)[...] = basis_ref[...].astype(BF16)
+    loads[0].wait()
+    wire = basis_ref[...].astype(BF16)
+    basis_rows(ga, q)[...] = wire
+    basis_rows(gb, p)[...] = wire
+    for c in loads[1:4]:
+        c.wait()
+    split_columns(lg_ref, lgs)
+    lgr[p] = lgs[p]
+
+    class Group:
+        def __init__(self, index, buffer, ring, pair, where):
+            self.index, self.buffer, self.ring, self.pair, self.where = index, buffer, ring, pair, where
+            self.sent = 0
+
+        def slot(self, step, other):
+            pair = (1 - self.pair) if other else self.pair
+            return ((self.ring + step) % 4) * 2 + pair
+
+        def half(self, slot, h):
+            return rows(self.buffer, slot * 2 + h, 16)
+
+        def copy(self, slot, h, to, n):
+            ref = self.half(slot, h)
+            return pltpu.make_async_remote_copy(
+                src_ref=ref, dst_ref=ref,
+                send_sem=gather_send.at[self.index, n], recv_sem=gather_recv.at[self.index, slot * 2 + h],
+                device_id=self.where(to), device_id_type=pl.DeviceIdType.MESH,
+            )
+
+        def send(self, slot, h, to):
+            c = self.copy(slot, h, to, self.sent)
+            self.sent += 1
+            c.start()
+            started.append(c)
+
+        def wait(self, step, other, h):
+            slot = self.slot(step, other)
+            self.copy(slot, h, self.slot(0, True), 0).wait_recv()
+            return slot
+
+        def own(self):
+            me_ = self.slot(0, False)
+            after, before, partner = self.slot(1, False), self.slot(3, False), self.slot(0, True)
+            self.send(me_, 0, after)
+            self.send(me_, 1, before)
+            self.send(me_, 0, partner)
+            self.send(me_, 1, partner)
+            self.send(me_, 0, before)
+            self.send(me_, 1, after)
+
+        def relay(self, other):
+            self.send(self.wait(3, other, 0), 0, self.slot(1, False))
+            self.send(self.wait(1, other, 1), 1, self.slot(3, False))
+
+        def partner(self):
+            slot = self.wait(0, True, 0)
+            self.send(slot, 0, self.slot(1, False))
+            self.send(slot, 0, self.slot(3, False))
+            slot = self.wait(0, True, 1)
+            self.send(slot, 1, self.slot(3, False))
+            self.send(slot, 1, self.slot(1, False))
+
+        def rest(self):
+            for other in (False, True):
+                self.wait(3, other, 1)
+                self.wait(1, other, 0)
+                self.wait(2, other, 0)
+                self.wait(2, other, 1)
+
+    by_q = Group(0, ga, z21, yh, lambda o: device(p, o))
+    by_p = Group(1, gb, x, z0, lambda o: device(o, q))
     pl.semaphore_wait(barrier, 14)
-    send_p(GB, lambda o: grad_ref, lambda i: rows(gb, i))
-    send_q(GA, lambda o: grad_ref, lambda i: rows(ga, i))
-    split_columns(lg_ref, lgs)
+    by_q.own()
+    by_p.own()
+    by_p.partner()
     send_p(LG, lambda o: lgs.at[o], lambda i: lgr.at[i])
-    send_q(WA, lambda o: rows(wa, q), lambda i: rows(wa, i))
-    send_p(WB, lambda o: rows(wb, p), lambda i: rows(wb, i))
-    rows(ga, q)[...] = grad_ref[...]
-    rows(gb, p)[...] = grad_ref[...]
-    lgr[p] = lgs[p]
-    wait_p(GB, lambda i: rows(gb, i))
-    wait_q(GA, lambda i: rows(ga, i))
+    by_p.relay(False)
+    by_q.relay(False)
+    by_q.partner()
+    by_p.relay(True)
+    by_q.relay(True)
+    by_p.rest()
+    by_q.rest()
     wait_p(LG, lambda i: lgr.at[i])
-    gram = dot(gb[...], ga[...], ((1,), (1,)))
+    gram = dot(gb[:, :D], ga[:, :D], ((1,), (1,)))
     new = 0.95 * lgr[...].reshape(256, 256) + 0.05 * gram
     gn[...] = new.reshape(8, R, 256)
     gback[p] = gn[p]
-    wait_q(WA, lambda i: rows(wa, i))
     high = new.astype(BF16)
     rest = new - high.astype(F32)
     mid = rest.astype(BF16)
     low = (rest - mid.astype(F32)).astype(BF16)
-    w = wa[...]
+    w = ga[:, D:]
     part = dot(high, w, ((1,), (0,))) + (dot(mid, w, ((1,), (0,))) + dot(low, w, ((1,), (0,))))
     pp[...] = part.reshape(8, R, K)
     send_p(PP, lambda o: pp.at[o], lambda i: pr.at[i])
     pr[p] = pp[p]
     wait_p(PP, lambda i: pr.at[i])
-    own = pr[0]
-    for i in range(1, 8):
-        own = own + pr[i]
+
+    def total(ref):
+        s = ref[0]
+        for i in range(1, 8):
+            s = s + ref[i]
+        return s
+
+    own = total(pr)
     rows(pb, p)[...] = own
     send_p(PG, lambda o: rows(pb, p), lambda i: rows(pb, i))
-    send_p(GN, lambda o: gn.at[o], lambda i: gback.at[i])
-    yf[...] = jnp.zeros_like(yf)
     yc[...] = jnp.zeros_like(yc)
     call[:, K:] = jnp.zeros((K, 128), F32)
     call[:, K : K + R] = own.T
-    wait_p(WB, lambda i: rows(wb, i))
     wait_p(PG, lambda i: rows(pb, i))
     pt[...] = pb[...].T
     left = rows(pt, p, 64)[...]
     fp[...] = dot(left, pb[...], ((1,), (0,)), HIGHEST).reshape(8, 8, K)
     send_q(FR, lambda o: fp.at[o], lambda i: fr.at[i])
-    cp[...] = dot(left, wb[...].astype(F32), ((1,), (0,)), HIGHEST).reshape(8, 8, K)
-    send_q(CR, lambda o: cp.at[o], lambda i: cr.at[i])
+    send_p(GN, lambda o: gn.at[o], lambda i: gback.at[i])
     fr[q] = fp[q]
+    cp[...] = dot(left, gb[:, D:].astype(F32), ((1,), (0,)), HIGHEST).reshape(8, 8, K)
     cr[q] = cp[q]
 
-    def total(ref):
-        s = ref[0]
-        for i in range(1, 8):
-            s = s + ref[i]
-        return s
+    def frow(i):
+        return rows(fall, i, 64)
 
     def crow(i, n=8):
         return call.at[pl.ds(pl.multiple_of(i * n, n), n), pl.ds(0, K)]
@@ -214,14 +301,11 @@
     wait_q(FR, lambda i: fr.at[i])
     rows(fall, p * 8 + q, 8)[...] = total(fr)
     send_q(FA, lambda o: rows(fall, p * 8 + q, 8), lambda i: rows(fall, p * 8 + i, 8))
-    wait_q(CR, lambda i: cr.at[i])
-    crow(p * 8 + q)[...] = total(cr)
-    send_q(CA, lambda o: crow(p * 8 + q), lambda i: crow(p * 8 + i))
     wait_q(FA, lambda i: rows(fall, p * 8 + i, 8))
-    send_p(FB, lambda o: rows(fall, p, 64), lambda i: rows(fall, i, 64))
+    send_p(FB, lambda o: frow(p), frow)
+    send_q(CR, lambda o: cp.at[o], lambda i: cr.at[i])
     wait_p(GN, lambda i: gback.at[i])
     join_columns(gback, lgn_ref)
-    wait_q(CA, lambda i: crow(p * 8 + i))
 
     def wait_row(phase, ref, i):
         @pl.when(i != p)
@@ -231,21 +315,22 @@
     scale = math.sqrt(D)
 
     def block(k):
-        return pl.ds(pl.multiple_of(k * 128, 128), 128)
-
-    def main_rows(k):
-        here = block(k)
-        u = yf[:, here]
-        a = fall[here, :] - dot(u, yf[...], ((0,), (0,)), HIGHEST)
-        diag[...] = fall[here, here] - dot(u, u, ((0,), (0,)), HIGHEST)
-        out = inverse_factor([diag[8 * i : 8 * i + 8, :] for i in range(16)])
-        for i in range(16):
-            inverse[k, 8 * i : 8 * i + 8, :] = out[i]
-        yf[here, :] = dot(inverse[k], a, ((1,), (0,)), HIGHEST)
+        return slice(k * 128, (k + 1) * 128)
+
+    def cross_reduced():
+        wait_q(CR, lambda i: cr.at[i])
+        crow(p * 8 + q)[...] = total(cr)
+        send_q(CA, lambda o: crow(p * 8 + q), lambda i: crow(p * 8 + i))
+
+    def cross_shared():
+        wait_q(CA, lambda i: crow(p * 8 + i))
+        send_p(CB, lambda o: crow(p, 64), lambda i: crow(i, 64))
 
     def side_rows(k):
         here = block(k)
-        a = call[here, :] - dot3(yf[:, here], yc[...], ((0,), (0,)))
+        a = call[here, :]
+        if k:
+            a = a - dot3(yf[: k * 128, here], yc[: k * 128, :], ((0,), (0,)))
         y = dot3(inverse[k], a, ((1,), (0,)))
         yc[here, :] = y
         basis_out[:, here] = (scale * y[:, K:]).T[:R, :]
@@ -253,32 +338,37 @@
         avg_out[:, here] = dot3(avg_ref[...], rotation, ((1,), (1,)))
         sq_out[:, here] = dot3(sq_ref[...], rotation * rotation, ((1,), (1,)))
 
-    @pl.loop(0, 2)
-    def _(k):
-        wait_row(FB, lambda i: rows(fall, i, 64), 2 * k)
-        wait_row(FB, lambda i: rows(fall, i, 64), 2 * k + 1)
-
-        @pl.when(k == 0)
-        def _():
-            for o in p_peers():
-                copy(CB, crow(p, 64), crow(p, 64), o, p, device(o, q)).start()
-
-        main_rows(k)
-
-    @pl.loop(2, 4)
-    def _(k):
-        for h in range(2):
-            wait_row(FB, lambda i: rows(fall, i, 64), 2 * k + h)
-            wait_row(CB, lambda i: crow(i, 64), 2 * (k - 2) + h)
-        side_rows(k - 2)
-        main_rows(k)
-
-    for h in range(4, 8):
-        wait_row(CB, lambda i: crow(i, 64), h)
-    side_rows(2)
-    side_rows(3)
-    for o in p_peers():
-        copy(CB, crow(p, 64), crow(p, 64), o, p, device(o, q)).wait_send()
+    hooks = {(0, 2): cross_reduced, (1, 0): cross_shared}
+    for k in range(4):
+        here = block(k)
+        for i in (2 * k, 2 * k + 1):
+            wait_row(FB, frow, i)
+        if k == 3:
+            for c in loads[4:]:
+                c.wait()
+            for i in (0, 1):
+                wait_row(CB, lambda j: crow(j, 64), i)
+        a = fall[here, k * 128 :]
+        d = fall[here, here]
+        if k:
+            u = yf[: k * 128, here]
+            d = d - dot(u, u, ((0,), (0,)), HIGHEST)
+        diag[...] = d
+        if k:
+            a = a - dot(u, yf[: k * 128, k * 128 :], ((0,), (0,)), HIGHEST)
+        if k == 3:
+            side_rows(0)
+        out = inverse_factor(
+            [diag[8 * i : 8 * i + 8, :] for i in range(16)], {m: f for (j, m), f in hooks.items() if j == k}
+        )
+        for i in range(16):
+            inverse[k, 8 * i : 8 * i + 8, :] = out[i]
+        if k < 3:
+            yf[here, k * 128 :] = dot(inverse[k], a, ((1,), (0,)), HIGHEST)
+    for i in range(2, 8):
+        wait_row(CB, lambda j: crow(j, 64), i)
+    for k in (1, 2, 3):
+        side_rows(k)
     for c in started:
         c.wait_send()
 
@@ -289,11 +379,11 @@
     return pl.pallas_call(
         kernel,
         out_shape=(sds((R, D), F32), sds((R, K), F32), sds((R, K), F32), sds((R, K), F32)),
-        in_specs=[vm] * 5,
+        in_specs=[pl.BlockSpec(memory_space=pltpu.HBM)] * 5,
         out_specs=(vm,) * 4,
         scratch_shapes=[
-            pltpu.VMEM((256, D), BF16), pltpu.VMEM((256, D), BF16),
-            pltpu.VMEM((256, K), BF16), pltpu.VMEM((256, K), BF16),
+            pltpu.VMEM((R, D), F32), pltpu.VMEM((R, K), F32), pltpu.VMEM((R, K), F32), pltpu.VMEM((R, K), F32),
+            pltpu.VMEM((256, WIDE), BF16), pltpu.VMEM((256, WIDE), BF16),
             pltpu.VMEM((8, R, 256), F32), pltpu.VMEM((8, R, 256), F32),
             pltpu.VMEM((8, R, 256), F32), pltpu.VMEM((8, R, 256), F32),
             pltpu.VMEM((8, R, K), F32), pltpu.VMEM((8, R, K), F32),
@@ -303,7 +393,8 @@
             pltpu.VMEM((K, K), F32), pltpu.VMEM((K, K + 128), F32),
             pltpu.VMEM((K, K), F32), pltpu.VMEM((K, K + 128), F32),
             pltpu.VMEM((128, 128), F32), pltpu.VMEM((4, 128, 128), F32),
-            pltpu.SemaphoreType.DMA((14, 8)), pltpu.SemaphoreType.DMA((14, 8)),
+            pltpu.SemaphoreType.DMA((10, 8)), pltpu.SemaphoreType.DMA((10, 8)),
+            pltpu.SemaphoreType.DMA((2, 14)), pltpu.SemaphoreType.DMA((2, 16)), pltpu.SemaphoreType.DMA((6,)),
         ],
         compiler_params=pltpu.CompilerParams(
             collective_id=0, has_side_effects=True, vmem_limit_bytes=48 * 1024 * 1024

time: 151 us -> 129 us (0.85)
  the two profiles are of different devices: /device:TPU:84 before, /device:TPU:6 now
where the time goes in v1:
time: 129 us; the launch traced here: 128 us
  Pallas kernels  120 us (93%)
  local copies, waits for them, and re-layouts  6.96 us (5%)
    pallas_call x1, Pallas kernels, body(): pl.pallas_call(kernel, out_shape=(sds((R, D), F32), sds((R, K), F32), sds...  120 us
    unnamed x14, local copies, waits for them, and re-layouts  6.96 us

profile of v1, /device:TPU:6, one launch (start us, length us, event | category | flops | bytes accessed | tf_op | source)
XLA Modules:
  0.0 127.8 jit_solution(6357291691861079442)
XLA Ops:
  0.6 0.0 copy-start
  0.6 0.9 copy-done
  1.6 0.0 copy-start.1
  1.6 0.9 copy-done.1
  2.5 0.0 copy-start.2
  2.5 0.8 copy-done.2
  3.3 0.0 copy-start.3
  3.3 0.8 copy-done.3
  4.2 0.0 copy-start.4
  4.2 0.8 copy-done.4
  5.0 120.2 %soap_refresh.1 = (f32[32,2048]{1,0:T(8,128)S(1)}, f32[32,512]{1,0:T(8,128)S(1)}, f32[32,512]{1,0:T(8,128)S(1)}, f32[32,512]{1,0:T(8,128)S(1)}) custom-call(bf16[32,2048]{1,0:T(8,128)(2,1)S(1)} %copy-done.1, f32[32,2048]{1,0:T(8,128)S(1)} %copy-done, f32[32,512]{1,0:T(8,128)S(1)} %copy-done.2, f32[32,512]{1,0:T(8,128)S(1)} %copy-done.3, f32[32,512]{1,0:T(8,128)S(1)} %copy-done.4), custom_call_target="tpu_custom_call" | custom-call | flops 1000000000 | bytes 2000000 | tf_op jit(solution)/shard_map/soap_refresh/pallas_call | solution.py:379
  125.2 0.7 copy.13
  125.9 0.6 copy.14
  126.5 0.6 copy.15
  127.1 0.6 copy.16
Async XLA Ops:
  0.6 1.0 copy-start
  1.6 0.9 copy-start.1
  2.5 0.8 copy-start.2
  3.3 0.8 copy-start.3
  4.2 0.8 copy-start.4

commit v2 on v1

--- a/solution.py
+++ b/solution.py
@@ -14,7 +14,7 @@
 HIGHEST = lax.Precision.HIGHEST
 F32 = jnp.float32
 BF16 = jnp.bfloat16
-LG, GN, PP, PG, FR, CR, FA, CA, FB, CB = range(10)
+LG, GN, PP, PG, R0, R1, A0, A1, FB, CR, CA, CB = 0, 1, 2, 3, 4, 5, 6, 7, 8, 12, 13, 14
 WIDE = D + K
 
 
@@ -99,7 +99,7 @@
     grad_hbm, lg_hbm, basis_hbm, avg_hbm, sq_hbm,
     lgn_ref, basis_out, avg_out, sq_out,
     lg_ref, basis_ref, avg_ref, sq_ref,
-    ga, gb, lgs, lgr, gn, gback, pp, pr, pb, pt, fp, fr, cp, cr, fall, call, yf, yc, diag, inverse,
+    ga, gb, lgs, lgr, gn, gback, pp, pr, pb, pt, fp, fr, cp, cr, fa, fall, call, yf, yc, diag, inverse,
     send_sem, recv_sem, gather_send, gather_recv, in_sem,
 ):
     me = lax.axis_index("dp")
@@ -279,56 +279,82 @@
     own = total(pr)
     rows(pb, p)[...] = own
     send_p(PG, lambda o: rows(pb, p), lambda i: rows(pb, i))
-    yc[...] = jnp.zeros_like(yc)
-    call[:, K:] = jnp.zeros((K, 128), F32)
-    call[:, K : K + R] = own.T
+    call[:, :, :, K:] = jnp.zeros((4, 8, 16, 128), F32)
+    own_t = own.T
+    for k in range(4):
+        for i in range(8):
+            at = k * 128 + i * 16
+            call[k, i, :, K : K + R] = own_t[at : at + 16]
     wait_p(PG, lambda i: rows(pb, i))
     pt[...] = pb[...].T
-    left = rows(pt, p, 64)[...]
-    fp[...] = dot(left, pb[...], ((1,), (0,)), HIGHEST).reshape(8, 8, K)
-    send_q(FR, lambda o: fp.at[o], lambda i: fr.at[i])
-    send_p(GN, lambda o: gn.at[o], lambda i: gback.at[i])
+    left = jnp.concatenate(
+        [pt[pl.ds(pl.multiple_of(k * 128 + p * 16, 16), 16), :] for k in range(4)], axis=0
+    )
+    part = dot(left, pb[...], ((1,), (0,)), HIGHEST)
+
+    def tiles(slot):
+        h, j = slot // 4, slot % 4
+        return [(0, h, j), (1, h, j + 1) if j < 3 else (3, h, 3), (2, h, 2 + j % 2)]
+
+    for slot in range(8):
+        for n, (k, h, c) in enumerate(tiles(slot)):
+            fp[slot, n] = part[k * 16 + h * 8 : k * 16 + h * 8 + 8, c * 128 : c * 128 + 128]
+    send_q(R0, lambda o: fp.at[o, pl.ds(0, 1)], lambda i: fr.at[i, pl.ds(0, 1)])
+    send_q(R1, lambda o: fp.at[o, pl.ds(1, 2)], lambda i: fr.at[i, pl.ds(1, 2)])
     fr[q] = fp[q]
     cp[...] = dot(left, gb[:, D:].astype(F32), ((1,), (0,)), HIGHEST).reshape(8, 8, K)
+    send_q(CR, lambda o: cp.at[o], lambda i: cr.at[i])
     cr[q] = cp[q]
 
-    def frow(i):
-        return rows(fall, i, 64)
-
-    def crow(i, n=8):
-        return call.at[pl.ds(pl.multiple_of(i * n, n), n), pl.ds(0, K)]
-
-    wait_q(FR, lambda i: fr.at[i])
-    rows(fall, p * 8 + q, 8)[...] = total(fr)
-    send_q(FA, lambda o: rows(fall, p * 8 + q, 8), lambda i: rows(fall, p * 8 + i, 8))
-    wait_q(FA, lambda i: rows(fall, p * 8 + i, 8))
-    send_p(FB, lambda o: frow(p), frow)
-    send_q(CR, lambda o: cp.at[o], lambda i: cr.at[i])
+    def frow(k):
+        return lambda i: fall.at[k, i, :, pl.ds(k * 128, K - k * 128)]
+
+    def c8(i):
+        return call.at[i // 2, p, pl.ds(pl.multiple_of((i % 2) * 8, 8), 8), pl.ds(0, K)]
+
+    def c64(i):
+        return call.at[:, i, :, pl.ds(0, K)]
+
+    wait_q(R0, lambda i: fr.at[i, pl.ds(0, 1)])
+    fa[q, 0] = total(fr.at[:, 0])
+    send_q(A0, lambda o: fa.at[q, pl.ds(0, 1)], lambda i: fa.at[i, pl.ds(0, 1)])
+    wait_q(R1, lambda i: fr.at[i, pl.ds(1, 2)])
+    for n in (1, 2):
+        fa[q, n] = total(fr.at[:, n])
+    send_q(A1, lambda o: fa.at[q, pl.ds(1, 2)], lambda i: fa.at[i, pl.ds(1, 2)])
+    send_p(GN, lambda o: gn.at[o], lambda i: gback.at[i])
+
+    def place(numbers):
+        for slot in range(8):
+            for n, (k, h, c) in enumerate(tiles(slot)):
+                if n in numbers and not (n == 2 and slot % 4 > 1):
+                    fall[k, p, h * 8 : h * 8 + 8, c * 128 : c * 128 + 128] = fa[slot, n]
+
+    wait_q(A0, lambda i: fa.at[i, pl.ds(0, 1)])
+    place((0,))
+    send_p(FB, lambda o: frow(0)(p), frow(0))
+    wait_q(A1, lambda i: fa.at[i, pl.ds(1, 2)])
+    place((1, 2))
+    for k in (1, 2, 3):
+        send_p(FB + k, lambda o: frow(k)(p), frow(k))
+    wait_q(CR, lambda i: cr.at[i])
+    c8(q)[...] = total(cr)
+    send_q(CA, lambda o: c8(q), c8)
     wait_p(GN, lambda i: gback.at[i])
     join_columns(gback, lgn_ref)
 
-    def wait_row(phase, ref, i):
-        @pl.when(i != p)
-        def _():
-            copy(phase, ref(i), ref(i), i, i, device(i, q)).wait_recv()
-
     scale = math.sqrt(D)
 
     def block(k):
         return slice(k * 128, (k + 1) * 128)
 
-    def cross_reduced():
-        wait_q(CR, lambda i: cr.at[i])
-        crow(p * 8 + q)[...] = total(cr)
-        send_q(CA, lambda o: crow(p * 8 + q), lambda i: crow(p * 8 + i))
-
     def cross_shared():
-        wait_q(CA, lambda i: crow(p * 8 + i))
-        send_p(CB, lambda o: crow(p, 64), lambda i: crow(i, 64))
+        wait_q(CA, c8)
+        send_p(CB, lambda o: c64(p), c64)
 
     def side_rows(k):
         here = block(k)
-        a = call[here, :]
+        a = call[k].reshape(128, K + 128)
         if k:
             a = a - dot3(yf[: k * 128, here], yc[: k * 128, :], ((0,), (0,)))
         y = dot3(inverse[k], a, ((1,), (0,)))
@@ -338,26 +364,25 @@
         avg_out[:, here] = dot3(avg_ref[...], rotation, ((1,), (1,)))
         sq_out[:, here] = dot3(sq_ref[...], rotation * rotation, ((1,), (1,)))
 
-    hooks = {(0, 2): cross_reduced, (1, 0): cross_shared}
+    def side_early():
+        for c in loads[4:]:
+            c.wait()
+        wait_p(CB, c64)
+        for k in (0, 1, 2):
+            side_rows(k)
+
+    hooks = {(0, 6): cross_shared, (3, 4): side_early}
     for k in range(4):
         here = block(k)
-        for i in (2 * k, 2 * k + 1):
-            wait_row(FB, frow, i)
-        if k == 3:
-            for c in loads[4:]:
-                c.wait()
-            for i in (0, 1):
-                wait_row(CB, lambda j: crow(j, 64), i)
-        a = fall[here, k * 128 :]
-        d = fall[here, here]
+        wait_p(FB + k, frow(k))
+        a = fall[k, :, :, k * 128 :].reshape(128, K - k * 128)
+        d = a[:, :128]
         if k:
             u = yf[: k * 128, here]
             d = d - dot(u, u, ((0,), (0,)), HIGHEST)
         diag[...] = d
         if k:
             a = a - dot(u, yf[: k * 128, k * 128 :], ((0,), (0,)), HIGHEST)
-        if k == 3:
-            side_rows(0)
         out = inverse_factor(
             [diag[8 * i : 8 * i + 8, :] for i in range(16)], {m: f for (j, m), f in hooks.items() if j == k}
         )
@@ -365,10 +390,7 @@
             inverse[k, 8 * i : 8 * i + 8, :] = out[i]
         if k < 3:
             yf[here, k * 128 :] = dot(inverse[k], a, ((1,), (0,)), HIGHEST)
-    for i in range(2, 8):
-        wait_row(CB, lambda j: crow(j, 64), i)
-    for k in (1, 2, 3):
-        side_rows(k)
+    side_rows(3)
     for c in started:
         c.wait_send()
 
@@ -388,16 +410,17 @@
             pltpu.VMEM((8, R, 256), F32), pltpu.VMEM((8, R, 256), F32),
             pltpu.VMEM((8, R, K), F32), pltpu.VMEM((8, R, K), F32),
             pltpu.VMEM((256, K), F32), pltpu.VMEM((K, 256), F32),
+            pltpu.VMEM((8, 3, 8, 128), F32), pltpu.VMEM((8, 3, 8, 128), F32),
             pltpu.VMEM((8, 8, K), F32), pltpu.VMEM((8, 8, K), F32),
-            pltpu.VMEM((8, 8, K), F32), pltpu.VMEM((8, 8, K), F32),
-            pltpu.VMEM((K, K), F32), pltpu.VMEM((K, K + 128), F32),
+            pltpu.VMEM((8, 3, 8, 128), F32),
+            pltpu.VMEM((4, 8, 16, K), F32), pltpu.VMEM((4, 8, 16, K + 128), F32),
             pltpu.VMEM((K, K), F32), pltpu.VMEM((K, K + 128), F32),
             pltpu.VMEM((128, 128), F32), pltpu.VMEM((4, 128, 128), F32),
-            pltpu.SemaphoreType.DMA((10, 8)), pltpu.SemaphoreType.DMA((10, 8)),
+            pltpu.SemaphoreType.DMA((15, 8)), pltpu.SemaphoreType.DMA((15, 8)),
             pltpu.SemaphoreType.DMA((2, 14)), pltpu.SemaphoreType.DMA((2, 16)), pltpu.SemaphoreType.DMA((6,)),
         ],
         compiler_params=pltpu.CompilerParams(
-            collective_id=0, has_side_effects=True, vmem_limit_bytes=48 * 1024 * 1024
+            collective_id=0, has_side_effects=True, vmem_limit_bytes=60 * 1024 * 1024
         ),
         cost_estimate=pl.CostEstimate(flops=1_000_000_000, bytes_accessed=2_000_000, transcendentals=0),
         name="soap_refresh",

time: 129 us -> 117 us (0.907)
  Pallas kernels: 120 us -> 112 us
  local copies, waits for them, and re-layouts: 6.96 us -> 4.06 us
    pallas_call x1, Pallas kernels: 120 us -> 112 us  [body(): pl.pallas_call(kernel, out_shape=(sds((R, D), F32), sds((R, K), F32), sds...]
    unnamed x14 -> x10, local copies, waits for them, and re-layouts: 6.96 us -> 4.06 us
where the time goes in v2:
time: 117 us
  Pallas kernels  112 us (96%)
  local copies, waits for them, and re-layouts  4.06 us (3%)
    pallas_call x1, Pallas kernels, body(): pl.pallas_call(kernel, out_shape=(sds((R, D), F32), sds((R, K), F32), sds...  112 us
    unnamed x10, local copies, waits for them, and re-layouts  4.06 us

profile of v2, /device:TPU:6, one launch (start us, length us, event | category | flops | bytes accessed | tf_op | source)
XLA Modules:
  0.0 116.6 jit_solution(10047011928169911153)
XLA Ops:
  0.6 111.9 %soap_refresh.1 = (f32[32,2048]{1,0:T(8,128)}, f32[32,512]{1,0:T(8,128)}, f32[32,512]{1,0:T(8,128)}, f32[32,512]{1,0:T(8,128)}) custom-call(bf16[32,2048]{1,0:T(8,128)(2,1)} %grad_hbm.1, f32[32,2048]{1,0:T(8,128)} %lg_hbm.1, f32[32,512]{1,0:T(8,128)} %basis_hbm.1, f32[32,512]{1,0:T(8,128)} %avg_hbm.1, f32[32,512]{1,0:T(8,128)} %sq_hbm.1), custom_call_target="tpu_custom_call" | custom-call | flops 1000000000 | bytes 2000000 | tf_op jit(solution)/shard_map/soap_refresh/pallas_call | solution.py:401
  112.5 0.0 copy-start.2
  112.5 1.7 %copy.13 = f32[32,2048]{1,0:T(8,128)} copy(f32[32,2048]{1,0:T(8,128)} %get-tuple-element.8) | data formatting | bytes 524288
  114.3 0.0 copy-done.2
  114.3 0.0 copy-start.1
  114.3 0.6 copy.14
  114.9 0.2 copy-done.1
  115.1 0.0 copy-start
  115.1 0.6 copy.15
  115.7 0.2 copy-done
  116.0 0.6 copy.16
Async XLA Ops:
  112.5 1.7 %copy-start.2 = (f32[32,512]{1,0:T(8,128)S(1)}, f32[32,512]{1,0:T(8,128)}, u32[]{:S(2)}) copy-start(f32[32,512]{1,0:T(8,128)} %get-tuple-element.9) | copy-start | bytes 196612
  114.3 0.9 copy-start.1
  115.1 0.9 copy-start

commit v3 on v2

--- a/solution.py
+++ b/solution.py
@@ -14,7 +14,7 @@
 HIGHEST = lax.Precision.HIGHEST
 F32 = jnp.float32
 BF16 = jnp.bfloat16
-LG, GN, PP, PG, R0, R1, A0, A1, FB, CR, CA, CB = 0, 1, 2, 3, 4, 5, 6, 7, 8, 12, 13, 14
+LG, GN, PP, PG, R0, R1, A0, A1, FB, CR, CA, CB = 0, 1, 2, 4, 6, 7, 8, 9, 10, 14, 15, 16
 WIDE = D + K
 
 
@@ -48,20 +48,28 @@
         r_m, s_m = a_rows[m], e_rows[m]
         c = [lane(r_m, 8 * m + t) for t in range(8)]
         v = jnp.zeros((8, 128), F32)
-        for t in range(8):
-            here = row == t
-            pivot = sub(c[t], t)
-            inv = 1.0 / pivot
-            s_t = sub(s_m, t)
-            v = jnp.where(here, s_t * lax.rsqrt(pivot), v)
-            mult = jnp.where(here, -1.0, c[t])
-            for u in range(t + 1, 8):
-                c[u] = jnp.where(here, 0.0, c[u]) - (mult * sub(c[u], t)) * inv
+        for t in range(0, 8, 2):
+            first, second, both = row == t, row == t + 1, row // 2 == t // 2
+            d00, d10, d11 = sub(c[t], t), sub(c[t], t + 1), sub(c[t + 1], t + 1)
+            det = d00 * d11 - d10 * d10
+            inv = 1.0 / det
+            m0 = jnp.where(first, -1.0, jnp.where(second, 0.0, c[t]))
+            m1 = jnp.where(first, 0.0, jnp.where(second, -1.0, c[t + 1]))
+            f0, f1 = m0 * d11 - m1 * d10, m1 * d00 - m0 * d10
+            s0, s1 = sub(s_m, t), sub(s_m, t + 1)
+            root = lax.rsqrt(d00)
+            v = jnp.where(first, s0 * root, v)
+            v = jnp.where(second, (d00 * s1 - d10 * s0) * (root * lax.rsqrt(det)), v)
+
+            def step(x, x0, x1):
+                return jnp.where(both, 0.0, x) - (f0 * x0 + f1 * x1) * inv
+
+            for u in range(t + 2, 8):
+                c[u] = step(c[u], sub(c[u], t), sub(c[u], t + 1))
             if m < n - 1:
-                r_m = jnp.where(here, 0.0, r_m) - (mult * sub(r_m, t)) * inv
-                s_m = jnp.where(here, 0.0, s_m) - (mult * s_t) * inv
-            elif t < 7:
-                s_m = jnp.where(here, 0.0, s_m) - (mult * s_t) * inv
+                r_m = step(r_m, sub(r_m, t), sub(r_m, t + 1))
+            if m < n - 1 or t < 6:
+                s_m = step(s_m, s0, s1)
         out.append(v)
         if m < n - 1:
             w = [sub(r_m, t) for t in range(8)]
@@ -97,11 +105,13 @@
 
 def kernel(
     grad_hbm, lg_hbm, basis_hbm, avg_hbm, sq_hbm,
-    lgn_ref, basis_out, avg_out, sq_out,
+    out_ref,
     lg_ref, basis_ref, avg_ref, sq_ref,
-    ga, gb, lgs, lgr, gn, gback, pp, pr, pb, pt, fp, fr, cp, cr, fa, fall, call, yf, yc, diag, inverse,
+    ga, gb, lgs, lgr, gn, gback, pp, pr, pb, pt, fp, fr, cp, cr, fa, fall, call, yf, yc, diag, inverse, avg_t, sq_t,
     send_sem, recv_sem, gather_send, gather_recv, in_sem,
 ):
+    lgn_ref = out_ref.at[:, pl.ds(0, D)]
+    basis_out, avg_out, sq_out = [out_ref.at[:, pl.ds(D + i * K, K)] for i in range(3)]
     me = lax.axis_index("dp")
     x, z21, z0, yh = me // 16, (me // 4) % 4, (me // 2) % 2, me % 2
     p = x * 2 + z0
@@ -175,10 +185,8 @@
     wire = basis_ref[...].astype(BF16)
     basis_rows(ga, q)[...] = wire
     basis_rows(gb, p)[...] = wire
-    for c in loads[1:4]:
+    for c in loads[1:3]:
         c.wait()
-    split_columns(lg_ref, lgs)
-    lgr[p] = lgs[p]
 
     class Group:
         def __init__(self, index, buffer, ring, pair, where):
@@ -221,6 +229,12 @@
             self.send(me_, 0, before)
             self.send(me_, 1, after)
 
+        def relay_top(self):
+            self.send(self.wait(3, True, 0), 0, self.slot(1, False))
+
+        def across(self):
+            self.send(self.wait(2, False, 1), 1, self.slot(0, True))
+
         def relay(self, other):
             self.send(self.wait(3, other, 0), 0, self.slot(1, False))
             self.send(self.wait(1, other, 1), 1, self.slot(3, False))
@@ -233,12 +247,15 @@
             self.send(slot, 1, self.slot(3, False))
             self.send(slot, 1, self.slot(1, False))
 
-        def rest(self):
+        def rest(self, crossed):
             for other in (False, True):
                 self.wait(3, other, 1)
                 self.wait(1, other, 0)
                 self.wait(2, other, 0)
-                self.wait(2, other, 1)
+                if other and crossed:
+                    self.wait(1, other, 1)
+                if other or not crossed:
+                    self.wait(2, other, 1)
 
     by_q = Group(0, ga, z21, yh, lambda o: device(p, o))
     by_p = Group(1, gb, x, z0, lambda o: device(o, q))
@@ -246,14 +263,18 @@
     by_q.own()
     by_p.own()
     by_p.partner()
+    loads[3].wait()
+    split_columns(lg_ref, lgs)
+    lgr[p] = lgs[p]
     send_p(LG, lambda o: lgs.at[o], lambda i: lgr.at[i])
     by_p.relay(False)
     by_q.relay(False)
     by_q.partner()
+    by_q.across()
     by_p.relay(True)
-    by_q.relay(True)
-    by_p.rest()
-    by_q.rest()
+    by_q.relay_top()
+    by_p.rest(False)
+    by_q.rest(True)
     wait_p(LG, lambda i: lgr.at[i])
     gram = dot(gb[:, :D], ga[:, :D], ((1,), (1,)))
     new = 0.95 * lgr[...].reshape(256, 256) + 0.05 * gram
@@ -263,30 +284,38 @@
     rest = new - high.astype(F32)
     mid = rest.astype(BF16)
     low = (rest - mid.astype(F32)).astype(BF16)
-    w = ga[:, D:]
-    part = dot(high, w, ((1,), (0,))) + (dot(mid, w, ((1,), (0,))) + dot(low, w, ((1,), (0,))))
-    pp[...] = part.reshape(8, R, K)
-    send_p(PP, lambda o: pp.at[o], lambda i: pr.at[i])
-    pr[p] = pp[p]
-    wait_p(PP, lambda i: pr.at[i])
-
     def total(ref):
         s = ref[0]
         for i in range(1, 8):
             s = s + ref[i]
         return s
 
-    own = total(pr)
-    rows(pb, p)[...] = own
-    send_p(PG, lambda o: rows(pb, p), lambda i: rows(pb, i))
+    def half(ref, i, h):
+        return ref.at[i, :, pl.ds(h * 256, 256)]
+
+    def rows_half(i, h):
+        return pb.at[pl.ds(pl.multiple_of(i * R, R), R), pl.ds(h * 256, 256)]
+
+    for h in range(2):
+        w = ga[:, D + h * 256 : D + h * 256 + 256]
+        part = dot(high, w, ((1,), (0,))) + (dot(mid, w, ((1,), (0,))) + dot(low, w, ((1,), (0,))))
+        pp[:, :, h * 256 : h * 256 + 256] = part.reshape(8, R, 256)
+        send_p(PP + h, lambda o: half(pp, o, h), lambda i: half(pr, i, h))
+    pr[p] = pp[p]
+    for h in range(2):
+        wait_p(PP + h, lambda i: half(pr, i, h))
+        rows_half(p, h)[...] = total(pr.at[:, :, pl.ds(h * 256, 256)])
+        send_p(PG + h, lambda o: rows_half(p, h), lambda i: rows_half(i, h))
+    own = rows(pb, p)[...]
     call[:, :, :, K:] = jnp.zeros((4, 8, 16, 128), F32)
     own_t = own.T
     for k in range(4):
         for i in range(8):
             at = k * 128 + i * 16
             call[k, i, :, K : K + R] = own_t[at : at + 16]
-    wait_p(PG, lambda i: rows(pb, i))
-    pt[...] = pb[...].T
+    for h in range(2):
+        wait_p(PG + h, lambda i: rows_half(i, h))
+        pt[h * 256 : h * 256 + 256, :] = pb[:, h * 256 : h * 256 + 256].T
     left = jnp.concatenate(
         [pt[pl.ds(pl.multiple_of(k * 128 + p * 16, 16), 16), :] for k in range(4)], axis=0
     )
@@ -312,7 +341,7 @@
     def c8(i):
         return call.at[i // 2, p, pl.ds(pl.multiple_of((i % 2) * 8, 8), 8), pl.ds(0, K)]
 
-    def c64(i):
+    def crows(i):
         return call.at[:, i, :, pl.ds(0, K)]
 
     wait_q(R0, lambda i: fr.at[i, pl.ds(0, 1)])
@@ -340,8 +369,13 @@
     wait_q(CR, lambda i: cr.at[i])
     c8(q)[...] = total(cr)
     send_q(CA, lambda o: c8(q), c8)
+    for c in loads[4:]:
+        c.wait()
     wait_p(GN, lambda i: gback.at[i])
     join_columns(gback, lgn_ref)
+    for source, turned in ((avg_ref, avg_t), (sq_ref, sq_t)):
+        turned[...] = jnp.zeros((K, 128), F32)
+        turned[:, :R] = source[...].T
 
     scale = math.sqrt(D)
 
@@ -349,48 +383,71 @@
         return slice(k * 128, (k + 1) * 128)
 
     def cross_shared():
+        for k in (1, 2, 3):
+            wait_p(FB + k, frow(k))
         wait_q(CA, c8)
-        send_p(CB, lambda o: c64(p), c64)
-
-    def side_rows(k):
+        send_p(CB, lambda o: crows(p), crows)
+
+    def tile_of(k, first, last):
+        return fall[k, :, :, first * 128 : last * 128].reshape(128, (last - first) * 128) * unit
+
+    state = {}
+
+    def side_before(k):
         here = block(k)
         a = call[k].reshape(128, K + 128)
         if k:
             a = a - dot3(yf[: k * 128, here], yc[: k * 128, :], ((0,), (0,)))
-        y = dot3(inverse[k], a, ((1,), (0,)))
+        yc[here, :] = a
+
+    def side_after(k):
+        here = block(k)
+        y = dot3(inverse[k], yc[here, :], ((1,), (0,)))
         yc[here, :] = y
-        basis_out[:, here] = (scale * y[:, K:]).T[:R, :]
-        rotation = y[:, :K] / scale
-        avg_out[:, here] = dot3(avg_ref[...], rotation, ((1,), (1,)))
-        sq_out[:, here] = dot3(sq_ref[...], rotation * rotation, ((1,), (1,)))
-
-    def side_early():
-        for c in loads[4:]:
-            c.wait()
-        wait_p(CB, c64)
-        for k in (0, 1, 2):
-            side_rows(k)
-
-    hooks = {(0, 6): cross_shared, (3, 4): side_early}
+        basis_out[:, here] = (y[:, K:] * (scale * root)).T[:R, :]
+        rotation = y[:, :K] * (root / scale)
+        avg_out[:, here] = dot3(rotation, avg_t[...], ((1,), (0,))).T[:R, :]
+        sq_out[:, here] = dot3(rotation * rotation, sq_t[...], ((1,), (0,))).T[:R, :]
+
+    def side():
+        wait_p(CB, crows)
+        for k in range(3):
+            side_before(k)
+            side_after(k)
+        side_before(3)
+
+    def wide(k):
+        def run():
+            if k < 3:
+                yf[block(k - 1), (k + 1) * 128 :] = dot(inverse[k - 1], state["a"][:, 128:], ((1,), (0,)), HIGHEST)
+                u = yf[: k * 128, block(k)]
+                state["a"] = tile_of(k, k + 1, 4) - dot(u, yf[: k * 128, (k + 1) * 128 :], ((0,), (0,)), HIGHEST)
+                v = yf[: k * 128, block(k + 1)]
+                state["d"] = tile_of(k + 1, k + 1, k + 2) - dot(v, v, ((0,), (0,)), HIGHEST)
+        return run
+
+    hooks = {
+        (0, 6): cross_shared, (1, 2): wide(1), (2, 2): wide(2),
+        (3, 4): side,
+    }
+    wait_p(FB, frow(0))
+    unit = 1.0 / fall[0, 0, 0:1, 0:1]
+    root = jnp.sqrt(unit)
+    diag[...] = tile_of(0, 0, 1)
     for k in range(4):
         here = block(k)
-        wait_p(FB + k, frow(k))
-        a = fall[k, :, :, k * 128 :].reshape(128, K - k * 128)
-        d = a[:, :128]
-        if k:
-            u = yf[: k * 128, here]
-            d = d - dot(u, u, ((0,), (0,)), HIGHEST)
-        diag[...] = d
-        if k:
-            a = a - dot(u, yf[: k * 128, k * 128 :], ((0,), (0,)), HIGHEST)
         out = inverse_factor(
             [diag[8 * i : 8 * i + 8, :] for i in range(16)], {m: f for (j, m), f in hooks.items() if j == k}
         )
         for i in range(16):
             inverse[k, 8 * i : 8 * i + 8, :] = out[i]
         if k < 3:
-            yf[here, k * 128 :] = dot(inverse[k], a, ((1,), (0,)), HIGHEST)
-    side_rows(3)
+            if k == 0:
+                state["a"], state["d"] = tile_of(0, 1, 4), tile_of(1, 1, 2)
+            t = dot(inverse[k], state["a"][:, :128], ((1,), (0,)), HIGHEST)
+            yf[here, block(k + 1)] = t
+            diag[...] = state["d"] - dot(t, t, ((0,), (0,)), HIGHEST)
+    side_after(3)
     for c in started:
         c.wait_send()
 
@@ -398,11 +455,11 @@
 def body(grad, left_gram, basis, exp_avg, exp_avg_sq):
     vm = pl.BlockSpec(memory_space=pltpu.VMEM)
     sds = jax.ShapeDtypeStruct
-    return pl.pallas_call(
+    both = pl.pallas_call(
         kernel,
-        out_shape=(sds((R, D), F32), sds((R, K), F32), sds((R, K), F32), sds((R, K), F32)),
+        out_shape=sds((R, D + 3 * K), F32),
         in_specs=[pl.BlockSpec(memory_space=pltpu.HBM)] * 5,
-        out_specs=(vm,) * 4,
+        out_specs=vm,
         scratch_shapes=[
             pltpu.VMEM((R, D), F32), pltpu.VMEM((R, K), F32), pltpu.VMEM((R, K), F32), pltpu.VMEM((R, K), F32),
             pltpu.VMEM((256, WIDE), BF16), pltpu.VMEM((256, WIDE), BF16),
@@ -416,7 +473,8 @@
             pltpu.VMEM((4, 8, 16, K), F32), pltpu.VMEM((4, 8, 16, K + 128), F32),
             pltpu.VMEM((K, K), F32), pltpu.VMEM((K, K + 128), F32),
             pltpu.VMEM((128, 128), F32), pltpu.VMEM((4, 128, 128), F32),
-            pltpu.SemaphoreType.DMA((15, 8)), pltpu.SemaphoreType.DMA((15, 8)),
+            pltpu.VMEM((K, 128), F32), pltpu.VMEM((K, 128), F32),
+            pltpu.SemaphoreType.DMA((20, 8)), pltpu.SemaphoreType.DMA((20, 8)),
             pltpu.SemaphoreType.DMA((2, 14)), pltpu.SemaphoreType.DMA((2, 16)), pltpu.SemaphoreType.DMA((6,)),
         ],
         compiler_params=pltpu.CompilerParams(
@@ -425,6 +483,7 @@
         cost_estimate=pl.CostEstimate(flops=1_000_000_000, bytes_accessed=2_000_000, transcendentals=0),
         name="soap_refresh",
     )(grad, left_gram, basis, exp_avg, exp_avg_sq)
+    return (both[:, :D],) + tuple(both[:, D + i * K : D + i * K + K] for i in range(3))
 
 
 def solution(mesh):

time: 117 us -> 114 us (0.974)
  Pallas kernels: 112 us -> 109 us
    unnamed x10 -> x0, local copies, waits for them, and re-layouts: 4.06 us -> none
    slice x0 -> x2, local copies, waits for them, and re-layouts: none -> 3.25 us  [the longest x1 1.67 us: body(): both[:, :D]]
    pallas_call x1, Pallas kernels: 112 us -> 109 us  [body(): pl.pallas_call(kernel, out_shape=sds((R, D + 3 * K), F32), in_specs=[pl.B...]
where the time goes in v3:
time: 114 us; the launch traced here: 113 us
  Pallas kernels  109 us (96%)
  local copies, waits for them, and re-layouts  3.25 us (3%)
    pallas_call x1, Pallas kernels, body(): pl.pallas_call(kernel, out_shape=sds((R, D + 3 * K), F32), in_specs=[pl.B...  109 us

profile of v3, /device:TPU:6, one launch (start us, length us, event | category | flops | bytes accessed | tf_op | source)
XLA Modules:
  0.0 113.4 jit_solution(17587412253732356624)
XLA Ops:
  0.6 109.5 %soap_refresh.1 = f32[32,3584]{1,0:T(8,128)} custom-call(bf16[32,2048]{1,0:T(8,128)(2,1)} %grad_hbm.1, f32[32,2048]{1,0:T(8,128)} %lg_hbm.1, f32[32,512]{1,0:T(8,128)} %basis_hbm.1, f32[32,512]{1,0:T(8,128)} %avg_hbm.1, f32[32,512]{1,0:T(8,128)} %sq_hbm.1), custom_call_target="tpu_custom_call" | custom-call | flops 1000000000 | bytes 2000000 | tf_op jit(solution)/shard_map/soap_refresh/pallas_call | solution.py:458
  110.1 1.6 %fusion = (f32[32,512]{1,0:T(8,128)}, f32[32,512]{1,0:T(8,128)}, f32[32,512]{1,0:T(8,128)}) fusion(f32[32,3584]{1,0:T(8,128)} %soap_refresh.1), kind=kLoop, calls=%fused_computation | loop fusion | bytes 393216 | tf_op jit(solution)/shard_map/slice | solution.py:486
  111.7 1.7 %slice.12 = f32[32,2048]{1,0:T(8,128)} slice(f32[32,3584]{1,0:T(8,128)} %soap_refresh.1), slice={[0:32], [0:2048]} | slice | bytes 524288 | tf_op jit(solution)/shard_map/slice | solution.py:486

commit v4 on v3

--- a/solution.py
+++ b/solution.py
@@ -229,32 +229,27 @@
             self.send(me_, 0, before)
             self.send(me_, 1, after)
 
-        def relay_top(self):
-            self.send(self.wait(3, True, 0), 0, self.slot(1, False))
-
-        def across(self):
-            self.send(self.wait(2, False, 1), 1, self.slot(0, True))
+        def across(self, h):
+            self.send(self.wait(2, False, h), h, self.slot(0, True))
 
         def relay(self, other):
             self.send(self.wait(3, other, 0), 0, self.slot(1, False))
             self.send(self.wait(1, other, 1), 1, self.slot(3, False))
 
-        def partner(self):
-            slot = self.wait(0, True, 0)
-            self.send(slot, 0, self.slot(1, False))
-            self.send(slot, 0, self.slot(3, False))
-            slot = self.wait(0, True, 1)
-            self.send(slot, 1, self.slot(3, False))
-            self.send(slot, 1, self.slot(1, False))
+        def partner(self, h):
+            slot = self.wait(0, True, h)
+            self.send(slot, h, self.slot(1 + 2 * h, False))
+            self.send(slot, h, self.slot(3 - 2 * h, False))
 
         def rest(self, crossed):
             for other in (False, True):
                 self.wait(3, other, 1)
                 self.wait(1, other, 0)
-                self.wait(2, other, 0)
                 if other and crossed:
+                    self.wait(3, other, 0)
                     self.wait(1, other, 1)
                 if other or not crossed:
+                    self.wait(2, other, 0)
                     self.wait(2, other, 1)
 
     by_q = Group(0, ga, z21, yh, lambda o: device(p, o))
@@ -262,17 +257,19 @@
     pl.semaphore_wait(barrier, 14)
     by_q.own()
     by_p.own()
-    by_p.partner()
+    by_q.relay(False)
+    by_p.partner(0)
+    by_p.partner(1)
     loads[3].wait()
     split_columns(lg_ref, lgs)
     lgr[p] = lgs[p]
     send_p(LG, lambda o: lgs.at[o], lambda i: lgr.at[i])
     by_p.relay(False)
-    by_q.relay(False)
-    by_q.partner()
-    by_q.across()
+    by_q.partner(0)
     by_p.relay(True)
-    by_q.relay_top()
+    by_q.across(0)
+    by_q.partner(1)
+    by_q.across(1)
     by_p.rest(False)
     by_q.rest(True)
     wait_p(LG, lambda i: lgr.at[i])
@@ -341,8 +338,8 @@
     def c8(i):
         return call.at[i // 2, p, pl.ds(pl.multiple_of((i % 2) * 8, 8), 8), pl.ds(0, K)]
 
-    def crows(i):
-        return call.at[:, i, :, pl.ds(0, K)]
+    def crows(h):
+        return lambda i: call.at[pl.ds(2 * h, 2), i, :, pl.ds(0, K)]
 
     wait_q(R0, lambda i: fr.at[i, pl.ds(0, 1)])
     fa[q, 0] = total(fr.at[:, 0])
@@ -362,13 +359,13 @@
     wait_q(A0, lambda i: fa.at[i, pl.ds(0, 1)])
     place((0,))
     send_p(FB, lambda o: frow(0)(p), frow(0))
+    wait_q(CR, lambda i: cr.at[i])
+    c8(q)[...] = total(cr)
+    send_q(CA, lambda o: c8(q), c8)
     wait_q(A1, lambda i: fa.at[i, pl.ds(1, 2)])
     place((1, 2))
     for k in (1, 2, 3):
         send_p(FB + k, lambda o: frow(k)(p), frow(k))
-    wait_q(CR, lambda i: cr.at[i])
-    c8(q)[...] = total(cr)
-    send_q(CA, lambda o: c8(q), c8)
     for c in loads[4:]:
         c.wait()
     wait_p(GN, lambda i: gback.at[i])
@@ -386,7 +383,8 @@
         for k in (1, 2, 3):
             wait_p(FB + k, frow(k))
         wait_q(CA, c8)
-        send_p(CB, lambda o: crows(p), crows)
+        for h in range(2):
+            send_p(CB + h, lambda o: crows(h)(p), crows(h))
 
     def tile_of(k, first, last):
         return fall[k, :, :, first * 128 : last * 128].reshape(128, (last - first) * 128) * unit
@@ -409,12 +407,15 @@
         avg_out[:, here] = dot3(rotation, avg_t[...], ((1,), (0,))).T[:R, :]
         sq_out[:, here] = dot3(rotation * rotation, sq_t[...], ((1,), (0,))).T[:R, :]
 
-    def side():
-        wait_p(CB, crows)
-        for k in range(3):
-            side_before(k)
-            side_after(k)
-        side_before(3)
+    def side(h):
+        def run():
+            wait_p(CB + h, crows(h))
+            side_before(2 * h)
+            side_after(2 * h)
+            side_before(2 * h + 1)
+            if h == 0:
+                side_after(1)
+        return run
 
     def wide(k):
         def run():
@@ -428,7 +429,7 @@
 
     hooks = {
         (0, 6): cross_shared, (1, 2): wide(1), (2, 2): wide(2),
-        (3, 4): side,
+        (3, 2): side(0), (3, 9): side(1),
     }
     wait_p(FB, frow(0))
     unit = 1.0 / fall[0, 0, 0:1, 0:1]

time: 114 us -> 110 us (0.965)
  Pallas kernels: 109 us -> 105 us
    pallas_call x1, Pallas kernels: 109 us -> 105 us  [body(): pl.pallas_call(kernel, out_shape=sds((R, D + 3 * K), F32), in_specs=[pl.B...]
where the time goes in v4:
time: 110 us; the launch traced here: 109 us
  Pallas kernels  105 us (95%)
  local copies, waits for them, and re-layouts  3.25 us (3%)
    pallas_call x1, Pallas kernels, body(): pl.pallas_call(kernel, out_shape=sds((R, D + 3 * K), F32), in_specs=[pl.B...  105 us

profile of v4, /device:TPU:6, one launch (start us, length us, event | category | flops | bytes accessed | tf_op | source)
XLA Modules:
  0.0 108.8 jit_solution(8006870550404726463)
XLA Ops:
  0.6 104.9 %soap_refresh.1 = f32[32,3584]{1,0:T(8,128)} custom-call(bf16[32,2048]{1,0:T(8,128)(2,1)} %grad_hbm.1, f32[32,2048]{1,0:T(8,128)} %lg_hbm.1, f32[32,512]{1,0:T(8,128)} %basis_hbm.1, f32[32,512]{1,0:T(8,128)} %avg_hbm.1, f32[32,512]{1,0:T(8,128)} %sq_hbm.1), custom_call_target="tpu_custom_call" | custom-call | flops 1000000000 | bytes 2000000 | tf_op jit(solution)/shard_map/soap_refresh/pallas_call | solution.py:459
  105.5 1.6 %fusion = (f32[32,512]{1,0:T(8,128)}, f32[32,512]{1,0:T(8,128)}, f32[32,512]{1,0:T(8,128)}) fusion(f32[32,3584]{1,0:T(8,128)} %soap_refresh.1), kind=kLoop, calls=%fused_computation | loop fusion | bytes 393216 | tf_op jit(solution)/shard_map/slice | solution.py:487
  107.1 1.7 %slice.12 = f32[32,2048]{1,0:T(8,128)} slice(f32[32,3584]{1,0:T(8,128)} %soap_refresh.1), slice={[0:32], [0:2048]} | slice | bytes 524288 | tf_op jit(solution)/shard_map/slice | solution.py:487

commit v5 on v4

--- a/solution.py
+++ b/solution.py
@@ -222,9 +222,9 @@
         def own(self):
             me_ = self.slot(0, False)
             after, before, partner = self.slot(1, False), self.slot(3, False), self.slot(0, True)
+            self.send(me_, 0, partner)
             self.send(me_, 0, after)
             self.send(me_, 1, before)
-            self.send(me_, 0, partner)
             self.send(me_, 1, partner)
             self.send(me_, 0, before)
             self.send(me_, 1, after)
@@ -329,7 +329,6 @@
     send_q(R1, lambda o: fp.at[o, pl.ds(1, 2)], lambda i: fr.at[i, pl.ds(1, 2)])
     fr[q] = fp[q]
     cp[...] = dot(left, gb[:, D:].astype(F32), ((1,), (0,)), HIGHEST).reshape(8, 8, K)
-    send_q(CR, lambda o: cp.at[o], lambda i: cr.at[i])
     cr[q] = cp[q]
 
     def frow(k):
@@ -344,6 +343,7 @@
     wait_q(R0, lambda i: fr.at[i, pl.ds(0, 1)])
     fa[q, 0] = total(fr.at[:, 0])
     send_q(A0, lambda o: fa.at[q, pl.ds(0, 1)], lambda i: fa.at[i, pl.ds(0, 1)])
+    send_q(CR, lambda o: cp.at[o], lambda i: cr.at[i])
     wait_q(R1, lambda i: fr.at[i, pl.ds(1, 2)])
     for n in (1, 2):
         fa[q, n] = total(fr.at[:, n])

time: 110 us -> 107 us (0.973)
  Pallas kernels: 105 us -> 102 us
    pallas_call x1, Pallas kernels: 105 us -> 102 us  [body(): pl.pallas_call(kernel, out_shape=sds((R, D + 3 * K), F32), in_specs=[pl.B...]
where the time goes in v5:
time: 107 us; the launch traced here: 106 us
  Pallas kernels  102 us (95%)
  local copies, waits for them, and re-layouts  3.25 us (3%)
    pallas_call x1, Pallas kernels, body(): pl.pallas_call(kernel, out_shape=sds((R, D + 3 * K), F32), in_specs=[pl.B...  102 us

profile of v5, /device:TPU:6, one launch (start us, length us, event | category | flops | bytes accessed | tf_op | source)
XLA Modules:
  0.0 105.5 jit_solution(5965793029596170133)
XLA Ops:
  0.6 101.6 %soap_refresh.1 = f32[32,3584]{1,0:T(8,128)} custom-call(bf16[32,2048]{1,0:T(8,128)(2,1)} %grad_hbm.1, f32[32,2048]{1,0:T(8,128)} %lg_hbm.1, f32[32,512]{1,0:T(8,128)} %basis_hbm.1, f32[32,512]{1,0:T(8,128)} %avg_hbm.1, f32[32,512]{1,0:T(8,128)} %sq_hbm.1), custom_call_target="tpu_custom_call" | custom-call | flops 1000000000 | bytes 2000000 | tf_op jit(solution)/shard_map/soap_refresh/pallas_call | solution.py:459
  102.3 1.6 %fusion = (f32[32,512]{1,0:T(8,128)}, f32[32,512]{1,0:T(8,128)}, f32[32,512]{1,0:T(8,128)}) fusion(f32[32,3584]{1,0:T(8,128)} %soap_refresh.1), kind=kLoop, calls=%fused_computation | loop fusion | bytes 393216 | tf_op jit(solution)/shard_map/slice | solution.py:487
  103.9 1.7 %slice.12 = f32[32,2048]{1,0:T(8,128)} slice(f32[32,3584]{1,0:T(8,128)} %soap_refresh.1), slice={[0:32], [0:2048]} | slice | bytes 524288 | tf_op jit(solution)/shard_map/slice | solution.py:487

commit v6 on v5

--- a/solution.py
+++ b/solution.py
@@ -379,9 +379,11 @@
     def block(k):
         return slice(k * 128, (k + 1) * 128)
 
-    def cross_shared():
+    def rows_here():
         for k in (1, 2, 3):
             wait_p(FB + k, frow(k))
+
+    def cross_shared():
         wait_q(CA, c8)
         for h in range(2):
             send_p(CB + h, lambda o: crows(h)(p), crows(h))
@@ -428,7 +430,7 @@
         return run
 
     hooks = {
-        (0, 6): cross_shared, (1, 2): wide(1), (2, 2): wide(2),
+        (0, 14): rows_here, (1, 3): cross_shared, (1, 2): wide(1), (2, 2): wide(2),
         (3, 2): side(0), (3, 9): side(1),
     }
     wait_p(FB, frow(0))

time: 107 us -> 108 us (level)
    pallas_call x1, Pallas kernels: 102 us -> 103 us  [body(): pl.pallas_call(kernel, out_shape=sds((R, D + 3 * K), F32), in_specs=[pl.B...]
where the time goes in v6:
time: 108 us; the launch traced here: 107 us
  Pallas kernels  103 us (95%)
  local copies, waits for them, and re-layouts  3.25 us (3%)
    pallas_call x1, Pallas kernels, body(): pl.pallas_call(kernel, out_shape=sds((R, D + 3 * K), F32), in_specs=[pl.B...  103 us

profile of v6, /device:TPU:6, one launch (start us, length us, event | category | flops | bytes accessed | tf_op | source)
XLA Modules:
  0.0 107.0 jit_solution(11448773468887103518)
XLA Ops:
  0.6 103.1 %soap_refresh.1 = f32[32,3584]{1,0:T(8,128)} custom-call(bf16[32,2048]{1,0:T(8,128)(2,1)} %grad_hbm.1, f32[32,2048]{1,0:T(8,128)} %lg_hbm.1, f32[32,512]{1,0:T(8,128)} %basis_hbm.1, f32[32,512]{1,0:T(8,128)} %avg_hbm.1, f32[32,512]{1,0:T(8,128)} %sq_hbm.1), custom_call_target="tpu_custom_call" | custom-call | flops 1000000000 | bytes 2000000 | tf_op jit(solution)/shard_map/soap_refresh/pallas_call | solution.py:461
  103.7 1.6 %fusion = (f32[32,512]{1,0:T(8,128)}, f32[32,512]{1,0:T(8,128)}, f32[32,512]{1,0:T(8,128)}) fusion(f32[32,3584]{1,0:T(8,128)} %soap_refresh.1), kind=kLoop, calls=%fused_computation | loop fusion | bytes 393216 | tf_op jit(solution)/shard_map/slice | solution.py:489
  105.3 1.7 %slice.12 = f32[32,2048]{1,0:T(8,128)} slice(f32[32,3584]{1,0:T(8,128)} %soap_refresh.1), slice={[0:32], [0:2048]} | slice | bytes 524288 | tf_op jit(solution)/shard_map/slice | solution.py:489
